TPU v7x, 32 devices: a whole 2x2x4 slice. The times are simulated.
32 devices in a mesh: area: 4 (over z), dev: 8 (over y, x, core).
Axes of the slice: x: 2, y: 2, z: 4, core: 2. Of those that a mesh axis runs over, the one named last changes fastest.
Arguments:
- wave_fwd: float32 [3, 16384, 128], P(None, ('area', 'dev')), may hold values from -6 to 6
- wave_bwd: float32 [3, 16384, 128], P(None, ('area', 'dev')), may hold values from -6 to 6
- seg_reflect: float32 [3, 16384], P(None, ('area', 'dev')), may hold values from 0.04 to 0.4
- seg_count: int32 [32, 64], P(('area', 'dev')), may hold values from 1 to 24, 512 in all within a row
- modal_admit: float32 [3, 2048], P(None, ('area', 'dev')), may hold values from 0.02 to 0.2
- modal_transform: float32 [3, 3], replicated, may hold values from -3.5 to 3.5
- end_slot: int32 [2048, 2], P(('area', 'dev')), may hold values from 0 to 255, as said below
- recv_bus: int32 [32, 256], P(('area', 'dev')), may hold values from -1 to 63, as said below
- bus_impedance: float32 [3, 3, 2048], P(None, None, ('area', 'dev')), as said below
- link_bus: int32 [192, 2], P('area'), may hold values from 0 to 511, as said below
- link_resist: float32 [192], P('area'), may hold values from 0.5 to 5
- source_current: float32 [4, 2048, 3, 128], P(None, ('area', 'dev')), may hold values from -6 to 6
Outputs:
- bus_voltage: float32 [4, 2048, 3, 128], P(None, ('area', 'dev'))
- final_fwd: float32 [3, 16384, 128], P(None, ('area', 'dev'))
- final_bwd: float32 [3, 16384, 128], P(None, ('area', 'dev'))
Inputs may be any that keep to these rules, and one draw needn't show every extreme that they name: `end_slot`: entry [l, s] is the slot of end s (0 sending, 1 receiving) of line l within its device's 32 blocks of 8 slots, block q // 8 going to owner device q // 8. The slots of one device are distinct. Every device fills all 8 slots of the block for some owner, and one owner receives 8 ends from every device. `recv_bus`: row r, column s * 8 + c: the local bus of device r to which slot c of device s's block for r attaches, and -1 exactly where no end of device s holds that slot. `link_bus`: the two buses of a link differ. `bus_impedance`: each bus's 3x3 matrix is symmetric with a positive diagonal larger than the sum of its row's other magnitudes.
All inputs are finite; a program needn't handle non-finite values.
Results may differ from a plain program's by a relative error of at most 0.00012.
Values sent between devices are 32-bit elements; how exact they have to be, the bound alone decides.
A program may use at most 64 MiB of HBM per device.

v0:
```python
import jax
import jax.numpy as jnp
from jax import lax
from jax.sharding import PartitionSpec as P

STEPS = 4


def solve_links(factor, rhs):
    lower = lax.linalg.triangular_solve(factor, rhs, left_side=True, lower=True)
    return lax.linalg.triangular_solve(factor, lower, left_side=True, lower=True, transpose_a=True)


def send_ends(rows):
    return lax.all_to_all(rows, ("area", "dev"), split_axis=0, concat_axis=0, tiled=True)


def return_volts(rows):
    return lax.all_to_all(rows, ("area", "dev"), split_axis=0, concat_axis=0, tiled=True)


def on_device(
    wave_fwd,
    wave_bwd,
    seg_reflect,
    seg_count,
    modal_admit,
    modal_transform,
    end_slot,
    recv_bus,
    bus_impedance,
    link_bus,
    link_resist,
    source_current,
):
    exact = lax.Precision.HIGHEST
    cases = wave_fwd.shape[2]
    line_total = end_slot.shape[0]
    counts = seg_count[0]
    first = jnp.cumsum(counts) - counts
    last = first + counts - 1
    bus_total = bus_impedance.shape[2]
    link_total = link_bus.shape[0]
    bus_index = jnp.arange(bus_total, dtype=jnp.int32) + lax.axis_index("dev") * bus_total
    incidence = (bus_index[:, None] == link_bus[None, :, 0]).astype(jnp.float32) - (
        bus_index[:, None] == link_bus[None, :, 1]
    ).astype(jnp.float32)
    partial_value = jnp.einsum(
        "bl,ijb,bm->limj", incidence, bus_impedance, incidence, precision=exact
    ).reshape(3 * link_total, 3 * link_total)
    matrix = lax.psum(partial_value, "dev") + jnp.diag(jnp.repeat(link_resist, 3))
    factor = jnp.linalg.cholesky(matrix)
    place_overall_sum = recv_bus.shape[1]
    one_hot = (jnp.arange(bus_total, dtype=jnp.int32)[:, None] == recv_bus).astype(jnp.float32)
    flat_slot = end_slot.reshape(-1)
    reflect_next = jnp.roll(seg_reflect, -1, axis=1)
    forward, backward = (wave_fwd, wave_bwd)
    voltages = []
    for step in range(STEPS):
        arriving = jnp.stack([backward[:, first, :], forward[:, last, :]], axis=2)
        history = 2.0 * jnp.einsum(
            "mi,mlsk->lsik",
            modal_transform,
            modal_admit[:, :, None, None] * arriving,
            precision=exact,
        )
        send_rows = (
            jnp.zeros((place_overall_sum, 3 * cases), jnp.float32)
            .at[flat_slot]
            .set(history.reshape(2 * line_total, 3 * cases))
        )
        received = send_ends(send_rows)
        summed = jnp.dot(
            one_hot, received, precision=exact, preferred_element_type=jnp.float32
        ).reshape(bus_total, 3, cases)
        inject = source_current[step] + summed
        open_volts = jnp.einsum("ijb,bjk->bik", bus_impedance, inject, precision=exact)
        sources = jnp.einsum("bl,bik->lik", incidence, open_volts, precision=exact).reshape(
            3 * link_total, cases
        )
        owned = lax.psum_scatter(sources, "dev", scatter_dimension=1, tiled=True)
        current = lax.all_gather(solve_links(factor, owned), "dev", axis=1, tiled=True)
        current = current.reshape(link_total, 3, cases)
        net = inject - jnp.einsum("bl,lik->bik", incidence, current, precision=exact)
        volts = jnp.einsum("ijb,bjk->bik", bus_impedance, net, precision=exact)
        voltages.append(volts)
        slot_volts = jnp.dot(
            one_hot.T,
            volts.reshape(bus_total, 3 * cases),
            precision=exact,
            preferred_element_type=jnp.float32,
        )
        back_rows = return_volts(slot_volts)
        end_volts = back_rows[flat_slot].reshape(line_total, 2, 3, cases)
        outgoing = (
            jnp.einsum("mi,lsik->mlsk", modal_transform, end_volts, precision=exact) - arriving
        )
        fwd_next = (1.0 - seg_reflect)[:, :, None] * jnp.roll(forward, 1, axis=1) + seg_reflect[
            :, :, None
        ] * backward
        fwd_next = fwd_next.at[:, first, :].set(outgoing[:, :, 0, :])
        bwd_next = (1.0 - reflect_next)[:, :, None] * jnp.roll(backward, -1, axis=1) + reflect_next[
            :, :, None
        ] * forward
        bwd_next = bwd_next.at[:, last, :].set(outgoing[:, :, 1, :])
        forward, backward = (fwd_next, bwd_next)
    return (jnp.stack(voltages), forward, backward)


def solution(mesh):
    in_specs = (
        P(None, ("area", "dev"), None),
        P(None, ("area", "dev"), None),
        P(None, ("area", "dev")),
        P(("area", "dev"), None),
        P(None, ("area", "dev")),
        P(),
        P(("area", "dev"), None),
        P(("area", "dev"), None),
        P(None, None, ("area", "dev")),
        P("area", None),
        P("area"),
        P(None, ("area", "dev"), None, None),
    )
    out_specs = (
        P(None, ("area", "dev"), None, None),
        P(None, ("area", "dev"), None),
        P(None, ("area", "dev"), None),
    )
    return jax.shard_map(
        on_device, mesh=mesh, in_specs=in_specs, out_specs=out_specs, check_vma=False
    )
```

profile of v0, /device:TPU:0, one launch (start us, length us, event | category | flops | bytes accessed | tf_op | source)
XLA Modules:
  0.0 490.9 jit_solution(10305870664416190752)
XLA Ops:
  16.4 7.4 %all-to-all-start = ((f32[32,8,384]{2,1,0:T(8,128)}), f32[32,8,384]{2,1,0:T(8,128)}, u32[]{:S(2)}, u32[]{:S(2)}) async-start(f32[32,8,384]{2,1,0:T(8,128)} %bitcast.11), calls=%async_computation | async-start | bytes 786432 | tf_op jit(solution)/shard_map/all_to_all | solution.py:15
  32.3 50.8 %all-reduce.7.cloned.1.call-done = f32[144,144]{1,0:T(8,128)} async-done(((f32[144,144]{1,0:T(8,128)}), f32[144,144]{1,0:T(8,128)}) %all-reduce.7.cloned.1.call-update) | async-done | bytes 82960 | tf_op jit(solution)/shard_map/psum | solution.py:51
  85.2 11.7 %cholesky.50 = f32[128,128]{1,0:T(8,128)S(1)} custom-call(f32[128,128]{1,0:T(8,128)S(1)} %cholesky.121), custom_call_target="Cholesky" | custom-call | tf_op jit(solution)/shard_map/jit(cholesky)/cholesky | solution.py:52
  97.0 9.8 %custom-call.17 = f32[1,128,128]{1,2,0:T(8,128)S(1)} custom-call(f32[1,128,128]{2,1,0:T(8,128)S(1)} %get-tuple-element.103), custom_call_target="InvertDiagBlocksLowerTriangular" | custom-call | tf_op jit(solution)/shard_map/jit(cholesky)/cholesky | solution.py:52
  115.5 19.7 %custom-call.25 = f32[2,128,128]{1,2,0:T(8,128)S(1)} custom-call(f32[2,128,128]{2,1,0:T(8,128)S(1)} %pad_maximum_fusion.9), custom_call_target="InvertDiagBlocksLowerTriangular" | custom-call | tf_op jit(solution)/shard_map/triangular_solve/custom-call.4 | solution.py:11
  135.2 14.8 %reduce-scatter.13.cloned.1.call-done = f32[16,144]{1,0:T(8,128)} async-done(((f32[128,144]{1,0:T(8,128)}), f32[16,144]{1,0:T(8,128)}) %reduce-scatter.13.cloned.1.call-update) | async-done | bytes 9232
  152.5 9.4 %all_gather.12 = f32[144,128]{0,1:T(8,128)S(1)} all-gather(f32[144,16]{0,1:T(8,128)S(1)} %pad_maximum_fusion.10), channel_id=1, replica_groups=mesh['area'=4,'dev'=8] {'dev'}, dimensions={1}, use_global_device_ids=true | all-gather | bytes 82944 | tf_op jit(solution)/shard_map/all_gather | solution.py:82
  164.1 4.6 all-to-all-start.1
  172.7 5.0 %fusion.5 = f32[3,512,128]{2,0,1:T(4,128)S(1)} fusion(f32[3,511,128]{2,0,1:T(4,128)} %copy.234, f32[3,1,128]{2,0,1:T(4,128)S(1)} %copy.235, f32[3,512]{0,1:T(8,128)S(1)} %copy.117, f32[3,512]{0,1:T(8,128)S(1)} %copy.114, f32[3,512,128]{2,1,0:T(8,128)S(1)} %copy-done.1), kind=kLoop, calls=%fused_computation.61 | loop fusion | flops 786432 | bytes 2371584 | tf_op jit(solution)/shard_map/add | solution.py:98
  177.7 4.5 fusion.4
  184.8 2.6 scatter_fusion.1
  188.1 2.6 scatter_fusion
  194.2 18.9 %all_to_all.84 = f32[32,8,384]{2,1,0:T(8,128)} all-to-all(f32[32,8,384]{2,1,0:T(8,128)S(1)} %bitcast.344), channel_id=1, replica_groups=mesh['area'=4,'dev'=8] {'area','dev'}, dimensions={0} | all-to-all | bytes 786432 | tf_op jit(solution)/shard_map/all_to_all | solution.py:15
  218.0 31.6 %reduce-scatter.15.cloned.1.call-done = f32[16,144]{1,0:T(8,128)} async-done(((f32[128,144]{1,0:T(8,128)}), f32[16,144]{1,0:T(8,128)}) %reduce-scatter.15.cloned.1.call-update) | async-done | bytes 9232
  253.4 9.4 %all_gather.13 = f32[144,128]{0,1:T(8,128)S(1)} all-gather(f32[144,16]{0,1:T(8,128)S(1)} %pad_maximum_fusion.11), channel_id=1, replica_groups=mesh['area'=4,'dev'=8] {'dev'}, dimensions={1}, use_global_device_ids=true | all-gather | bytes 82944 | tf_op jit(solution)/shard_map/all_gather | solution.py:82
  265.8 4.7 all-to-all-start.3
  271.0 3.2 fusion.7
  276.6 7.1 %all-to-all-done.3 = f32[32,8,384]{2,1,0:T(8,128)} async-done(((f32[32,8,384]{2,1,0:T(8,128)}), f32[32,8,384]{2,1,0:T(8,128)}, u32[]{:S(2)}, u32[]{:S(2)}) %all-to-all-start.3) | async-done | bytes 393248 | tf_op jit(solution)/shard_map/all_to_all | solution.py:19
  287.4 2.4 scatter_fusion.3
  295.8 15.6 %all_to_all.85 = f32[32,8,384]{2,1,0:T(8,128)S(1)} all-to-all(f32[32,8,384]{2,1,0:T(8,128)S(1)} %bitcast.347), channel_id=1, replica_groups=mesh['area'=4,'dev'=8] {'area','dev'}, dimensions={0} | all-to-all | bytes 786432 | tf_op jit(solution)/shard_map/all_to_all | solution.py:15
  314.6 31.5 %reduce-scatter.17.cloned.1.call-done = f32[16,144]{1,0:T(8,128)} async-done(((f32[128,144]{1,0:T(8,128)}), f32[16,144]{1,0:T(8,128)}) %reduce-scatter.17.cloned.1.call-update) | async-done | bytes 9232
  350.0 9.2 %all_gather.14 = f32[144,128]{0,1:T(8,128)S(1)} all-gather(f32[144,16]{0,1:T(8,128)S(1)} %pad_maximum_fusion.12), channel_id=1, replica_groups=mesh['area'=4,'dev'=8] {'dev'}, dimensions={1}, use_global_device_ids=true | all-gather | bytes 82944 | tf_op jit(solution)/shard_map/all_gather | solution.py:82
  361.4 4.7 all-to-all-start.5
  367.1 3.2 fusion.9
  372.7 6.7 %all-to-all-done.5 = f32[32,8,384]{2,1,0:T(8,128)} async-done(((f32[32,8,384]{2,1,0:T(8,128)}), f32[32,8,384]{2,1,0:T(8,128)}, u32[]{:S(2)}, u32[]{:S(2)}) %all-to-all-start.5) | async-done | bytes 393248 | tf_op jit(solution)/shard_map/all_to_all | solution.py:19
  391.4 15.6 %all_to_all.86 = f32[32,8,384]{2,1,0:T(8,128)S(1)} all-to-all(f32[32,8,384]{2,1,0:T(8,128)S(1)} %bitcast.342), channel_id=1, replica_groups=mesh['area'=4,'dev'=8] {'area','dev'}, dimensions={0} | all-to-all | bytes 786432 | tf_op jit(solution)/shard_map/all_to_all | solution.py:15
  413.7 28.0 %reduce-scatter.19.cloned.1.call-done = f32[16,144]{1,0:T(8,128)} async-done(((f32[128,144]{1,0:T(8,128)}), f32[16,144]{1,0:T(8,128)}) %reduce-scatter.19.cloned.1.call-update) | async-done | bytes 9232
  445.7 9.2 %all_gather.15 = f32[144,128]{0,1:T(8,128)S(1)} all-gather(f32[144,16]{0,1:T(8,128)S(1)} %pad_maximum_fusion.13), channel_id=1, replica_groups=mesh['area'=4,'dev'=8] {'dev'}, dimensions={1}, use_global_device_ids=true | all-gather | bytes 82944 | tf_op jit(solution)/shard_map/all_gather | solution.py:82
  457.8 4.8 all-to-all-start.7
  462.6 4.0 fusion.10
  466.6 3.7 fusion.11
  472.3 3.5 all-to-all-done.7
  (349 shorter events, 113.9 us)
Async XLA Ops:
  7.2 17.3 %copy-start.55 = (f32[3,3,64]{2,1,0:T(4,128)S(1)}, f32[3,3,64]{2,1,0:T(4,128)}, u32[]{:S(2)}) copy-start(f32[3,3,64]{2,1,0:T(4,128)} %param.24) | copy-start | bytes 6916
  16.4 94.9 %all-to-all-start = ((f32[32,8,384]{2,1,0:T(8,128)}), f32[32,8,384]{2,1,0:T(8,128)}, u32[]{:S(2)}, u32[]{:S(2)}) async-start(f32[32,8,384]{2,1,0:T(8,128)} %bitcast.11), calls=%async_computation | async-start | bytes 786432 | tf_op jit(solution)/shard_map/all_to_all | solution.py:15
  23.9 59.2 %all-reduce.7.cloned.1.call-start = ((), (), s32[]{:S(2)}) async-start(), calls=%async_computation.12 | async-start | bytes 294912 | tf_op jit(solution)/shard_map/psum | solution.py:51
  29.8 82.7 %copy-start.40 = (s32[1,256]{1,0:T(1,128)S(1)}, s32[1,256]{1,0:T(1,128)}, u32[]{:S(2)}) copy-start(s32[1,256]{1,0:T(1,128)} %param.23) | copy-start | bytes 3076
  29.8 84.5 %copy-start.43 = (s32[48]{0:T(128)S(1)}, s32[48]{0:T(128)}, u32[]{:S(2)}) copy-start(s32[48]{0:T(128)} %copy-done.42) | copy-start | bytes 580
  29.8 84.5 %copy-start.46 = (s32[48]{0:T(128)S(1)}, s32[48]{0:T(128)}, u32[]{:S(2)}) copy-start(s32[48]{0:T(128)} %copy-done.45) | copy-start | bytes 580
  29.8 84.5 %copy-start.49 = (s32[64]{0:T(128)S(1)}, s32[64]{0:T(128)}, u32[]{:S(2)}) copy-start(s32[64]{0:T(128)} %copy-done.48) | copy-start | bytes 772
  29.8 120.2 %reduce-scatter.13.cloned.1.call-start = ((), (), s32[]{:S(2)}) async-start(), calls=%async_computation.13 | async-start | bytes 147456
  85.2 83.6 %copy-start.69 = (s32[128]{0:T(128)S(1)}, s32[128]{0:T(128)}, u32[]{:S(2)}) copy-start(s32[128]{0:T(128)} %copy-done.68) | copy-start | bytes 1540
  96.9 71.9 %copy-start.2 = (f32[3,512,128]{2,1,0:T(8,128)S(1)}, f32[3,512,128]{2,1,0:T(8,128)}, u32[]{:S(2)}) copy-start(f32[3,512,128]{2,1,0:T(8,128)} %param.16) | copy-start | bytes 2359300
  96.9 72.1 %copy-start.1 = (f32[3,512,128]{2,1,0:T(8,128)S(1)}, f32[3,512,128]{2,1,0:T(8,128)}, u32[]{:S(2)}) copy-start(f32[3,512,128]{2,1,0:T(8,128)} %param.17) | copy-start | bytes 2359300
  111.2 52.9 %copy-start.28 = (f32[144,144]{1,0:T(8,128)}, f32[144,144]{1,0:T(8,128)S(1)}, u32[]{:S(2)}) copy-start(f32[144,144]{1,0:T(8,128)S(1)} %select_select_fusion) | copy-start | bytes 248836
  135.2 35.4 %copy-start.15 = (f32[2,128,128]{1,2,0:T(8,128)}, f32[2,128,128]{1,2,0:T(8,128)S(1)}, u32[]{:S(2)}) copy-start(f32[2,128,128]{1,2,0:T(8,128)S(1)} %custom-call.25) | copy-start | bytes 393220
  164.1 18.1 %all-to-all-start.1 = ((f32[32,8,384]{2,1,0:T(8,128)}), f32[32,8,384]{2,1,0:T(8,128)S(1)}, u32[]{:S(2)}, u32[]{:S(2)}) async-start(f32[32,8,384]{2,1,0:T(8,128)} %fusion.58), calls=%async_computation.1 | async-start | bytes 786432 | tf_op jit(solution)/shard_map/all_to_all | solution.py:19
  168.7 80.8 %reduce-scatter.15.cloned.1.call-start = ((), (), s32[]{:S(2)}) async-start(), calls=%async_computation.14 | async-start | bytes 147456
  172.7 98.1 %copy-start.9 = (f32[3,512]{0,1:T(8,128)}, f32[3,512]{0,1:T(8,128)S(1)}, u32[]{:S(2)}) copy-start(f32[3,512]{0,1:T(8,128)S(1)} %copy.109) | copy-start | bytes 18436
  182.2 32.1 %copy-start.41 = (s32[1,256]{1,0:T(1,128)S(1)}, s32[1,256]{1,0:T(1,128)}, u32[]{:S(2)}) copy-start(s32[1,256]{1,0:T(1,128)} %param.23) | copy-start | bytes 3076
  183.0 33.1 %copy-start.44 = (s32[48]{0:T(128)S(1)}, s32[48]{0:T(128)}, u32[]{:S(2)}) copy-start(s32[48]{0:T(128)} %copy-done.42) | copy-start | bytes 580
  183.0 33.1 %copy-start.47 = (s32[48]{0:T(128)S(1)}, s32[48]{0:T(128)}, u32[]{:S(2)}) copy-start(s32[48]{0:T(128)} %copy-done.45) | copy-start | bytes 580
  183.1 67.1 %copy-start.16 = (f32[2,128,128]{1,2,0:T(8,128)S(1)}, f32[2,128,128]{1,2,0:T(8,128)}, u32[]{:S(2)}) copy-start(f32[2,128,128]{1,2,0:T(8,128)} %copy-done.15) | copy-start | bytes 393220
  265.8 17.9 %all-to-all-start.3 = ((f32[32,8,384]{2,1,0:T(8,128)}), f32[32,8,384]{2,1,0:T(8,128)}, u32[]{:S(2)}, u32[]{:S(2)}) async-start(f32[32,8,384]{2,1,0:T(8,128)} %fusion.56), calls=%async_computation.3 | async-start | bytes 786432 | tf_op jit(solution)/shard_map/all_to_all | solution.py:19
  270.5 75.6 %reduce-scatter.17.cloned.1.call-start = ((), (), s32[]{:S(2)}) async-start(), calls=%async_computation.15 | async-start | bytes 147456
  285.6 27.8 %copy-start.50 = (s32[64]{0:T(128)S(1)}, s32[64]{0:T(128)}, u32[]{:S(2)}) copy-start(s32[64]{0:T(128)} %copy-done.48) | copy-start | bytes 772
  285.7 61.1 %copy-start.17 = (f32[2,128,128]{1,2,0:T(8,128)S(1)}, f32[2,128,128]{1,2,0:T(8,128)}, u32[]{:S(2)}) copy-start(f32[2,128,128]{1,2,0:T(8,128)} %copy-done.15) | copy-start | bytes 393220
  361.4 17.9 %all-to-all-start.5 = ((f32[32,8,384]{2,1,0:T(8,128)}), f32[32,8,384]{2,1,0:T(8,128)}, u32[]{:S(2)}, u32[]{:S(2)}) async-start(f32[32,8,384]{2,1,0:T(8,128)} %fusion.54), calls=%async_computation.5 | async-start | bytes 786432 | tf_op jit(solution)/shard_map/all_to_all | solution.py:19
  366.2 75.6 %reduce-scatter.19.cloned.1.call-start = ((), (), s32[]{:S(2)}) async-start(), calls=%async_computation.16 | async-start | bytes 147456
  381.3 27.8 %copy-start.51 = (s32[64]{0:T(128)S(1)}, s32[64]{0:T(128)}, u32[]{:S(2)}) copy-start(s32[64]{0:T(128)} %copy-done.48) | copy-start | bytes 772
  407.1 35.4 %copy-start.18 = (f32[2,128,128]{1,2,0:T(8,128)S(1)}, f32[2,128,128]{1,2,0:T(8,128)}, u32[]{:S(2)}) copy-start(f32[2,128,128]{1,2,0:T(8,128)} %copy-done.15) | copy-start | bytes 393220
  410.2 44.7 %copy-start.27 = (f32[64,3,128]{2,0,1:T(8,128)S(1)}, f32[64,3,128]{2,0,1:T(8,128)}, u32[]{:S(2)}) copy-start(f32[64,3,128]{2,0,1:T(8,128)} %copy-done.26) | copy-start | bytes 294916
  410.2 52.3 %copy-start.4 = (f32[3,512]{0,1:T(8,128)S(1)}, f32[3,512]{0,1:T(8,128)}, u32[]{:S(2)}) copy-start(f32[3,512]{0,1:T(8,128)} %copy-done.3) | copy-start | bytes 18436
  413.7 52.9 %copy-start.8 = (f32[3,512]{0,1:T(8,128)S(1)}, f32[3,512]{0,1:T(8,128)}, u32[]{:S(2)}) copy-start(f32[3,512]{0,1:T(8,128)} %copy-done.5) | copy-start | bytes 18436
  457.8 17.9 %all-to-all-start.7 = ((f32[32,8,384]{2,1,0:T(8,128)}), f32[32,8,384]{2,1,0:T(8,128)S(1)}, u32[]{:S(2)}, u32[]{:S(2)}) async-start(f32[32,8,384]{2,1,0:T(8,128)} %fusion.52), calls=%async_computation.7 | async-start | bytes 786432 | tf_op jit(solution)/shard_map/all_to_all | solution.py:19
  (49 other events, 334.8 us)
Sparse Core Ops, SparseCore 0:
  29.9 53.0 all-reduce.6
  115.6 34.3 reduce-scatter.12
  218.1 31.3 reduce-scatter.14
  314.7 31.3 reduce-scatter.16
  410.4 31.3 reduce-scatter.18
where the time goes:
time: 497 us; the launch traced here: 491 us
  waiting for transfers between devices  174 us (35%)
  blocking collectives  87.2 us (18%)
  other arithmetic  76.1 us (15%)
  local copies, waits for them, and re-layouts  69.5 us (14%)
  matrix products  39.5 us (8%)
  starting transfers between devices  27.3 us (5%)
  between operations  17.3 us (3%)
    unnamed x9, waiting for transfers between devices  106 us
    psum x1, waiting for transfers between devices, on_device(): lax.psum(partial_value, 'dev') + jnp.diag(jnp.repeat(link_resist, 3))  50.8 us
    all_to_all x3, blocking collectives, send_ends(): lax.all_to_all(rows, ('area', 'dev'), split_axis=0, concat_axis=0, tiled=...  50.2 us
    all_gather x4, blocking collectives, on_device(): lax.all_gather(solve_links(factor, owned), 'dev', axis=1, tiled=True)  37.1 us
    another operation x7, other arithmetic, on_device(): factor = jnp.linalg.cholesky(matrix)  24.3 us
    another operation x10, other arithmetic, solve_links(): lax.linalg.triangular_solve(factor, lower, left_side=True, lower=True, tr...  20 us
    all_to_all x4, starting transfers between devices, return_volts(): lax.all_to_all(rows, ('area', 'dev'), split_axis=0, concat_axis=0, tiled=...  18.8 us
    all_to_all x4, waiting for transfers between devices, return_volts(): lax.all_to_all(rows, ('area', 'dev'), split_axis=0, concat_axis=0, tiled=...  17.2 us
  transfers between devices with their start and end apart: 10, of which 8 were waited for; matrix products, arithmetic and copies ran while one was open for 19% of the time, Pallas kernels for 0%

commit v1 on v0

v1 whole, which is shorter than its diff:
```python
import functools

import jax
import jax.numpy as jnp
from jax import lax
from jax.experimental import pallas as pl
from jax.experimental.pallas import tpu as pltpu
from jax.sharding import PartitionSpec as P

STEPS = 4
MESH = pl.DeviceIdType.MESH
F32 = jnp.float32
BF16 = jnp.bfloat16
EXACT = lax.Precision.HIGHEST


def iota(shape, dim):
    return lax.broadcasted_iota(jnp.int32, shape, dim)


def to_column(row):
    n = row.shape[1]
    eye = iota((n, n), 0) == iota((n, n), 1)
    return jnp.sum(jnp.where(eye, row, 0.0), axis=1, keepdims=True)


def to_row(column):
    n = column.shape[0]
    eye = iota((n, n), 0) == iota((n, n), 1)
    return jnp.sum(jnp.where(eye, column, 0.0), axis=0, keepdims=True)


def onehot(flag):
    return jnp.where(flag, 1.0, 0.0).astype(BF16)


def pick(matrix, value):
    n = value.shape[1]
    high = value.astype(BF16)
    low = (value - high.astype(F32)).astype(BF16)
    both = jnp.dot(
        matrix, jnp.concatenate([high, low], axis=1), preferred_element_type=F32
    )
    return both[:, :n] + both[:, n:]


def kernel(
    areas,
    devs,
    link_real,
    fwd_in,
    bwd_in,
    refl_ref,
    count_ref,
    admit_ref,
    trans_ref,
    slot_ref,
    recv_ref,
    imp_ref,
    link_ref,
    resist_ref,
    src_ref,
    volt_ref,
    fwd,
    bwd,
    h_send,
    h_recv,
    e_send,
    e_recv,
    g_send,
    g_recv,
    v_send,
    v_recv,
    imp_all,
    gb,
    gf,
    gbt,
    gft,
    rsum,
    rback,
    ct,
    cm,
    adm,
    zcol,
    keep_f,
    take_f,
    keep_b,
    take_b,
    arr,
    inj,
    minv,
    send_sem,
    recv_sem,
    imp_sem,
):
    total = areas * devs
    area, dev = lax.axis_index("area"), lax.axis_index("dev")
    me = area * devs + dev
    cases = fwd.shape[2]
    segs = fwd.shape[1]
    lines = slot_ref.shape[0]
    slots = recv_ref.shape[1]
    buses = imp_ref.shape[1]
    links = link_ref.shape[0]
    cap = slots // total
    lp = links // devs

    barrier = pltpu.get_barrier_semaphore()

    def peer_of(p):
        peer = lax.rem(me + p, total)
        return peer, (peer // devs, lax.rem(peer, devs))

    @pl.loop(1, total)
    def _(p):
        _, where = peer_of(p)
        pl.semaphore_signal(barrier, inc=1, device_id=where, device_id_type=MESH)

    def push_all(send, recv, phase, step):
        @pl.loop(1, total)
        def _(p):
            peer, where = peer_of(p)
            pltpu.make_async_remote_copy(
                src_ref=send.at[step, peer],
                dst_ref=recv.at[step, me],
                send_sem=send_sem.at[phase, step],
                recv_sem=recv_sem.at[phase, step],
                device_id=where,
                device_id_type=MESH,
            ).start()

    def push_area(source, recv, phase, step):
        @pl.loop(1, devs)
        def _(p):
            other = lax.rem(dev + p, devs)
            pltpu.make_async_remote_copy(
                src_ref=source(other),
                dst_ref=recv.at[step, dev],
                send_sem=send_sem.at[phase, step],
                recv_sem=recv_sem.at[phase, step],
                device_id=(area, other),
                device_id_type=MESH,
            ).start()

    def wait(buf, count, sem):
        ref = buf.at[pl.ds(0, count)]
        pltpu.make_async_copy(ref, ref, sem).wait()

    counts_row = count_ref[...].astype(F32)
    counts_col = to_column(counts_row)
    square = (lines, lines)
    first_col = jnp.sum(
        jnp.where(iota(square, 1) < iota(square, 0), counts_row, 0.0), axis=1, keepdims=True
    )
    first_row = to_row(first_col)
    last_col = first_col + counts_col - 1.0
    last_row = first_row + counts_row - 1.0
    slot0_col = slot_ref[:, 0:1].astype(F32)
    slot1_col = slot_ref[:, 1:2].astype(F32)
    slot0_row, slot1_row = to_row(slot0_col), to_row(slot1_col)
    seg_lane = iota((lines, segs), 1).astype(F32)
    seg_sub = iota((segs, lines), 0).astype(F32)
    slot_lane = iota((lines, slots), 1).astype(F32)
    slot_sub = iota((slots, lines), 0).astype(F32)
    q0, q1 = onehot(slot_sub == slot0_row), onehot(slot_sub == slot1_row)
    gb[...] = jnp.dot(q0, onehot(seg_lane == first_col), preferred_element_type=F32).astype(BF16)
    gf[...] = jnp.dot(q1, onehot(seg_lane == last_col), preferred_element_type=F32).astype(BF16)
    held = q0.astype(F32) + q1.astype(F32)
    for m in range(3):
        column = 2.0 * jnp.sum(held * admit_ref[m : m + 1, :], axis=1, keepdims=True)
        adm[m] = jnp.broadcast_to(column, (slots, cases))

    def gather_send(step):
        for m in range(3):
            arr[m] = pick(gb[...], bwd[m]) + pick(gf[...], fwd[m])
        for i in range(3):
            value = trans_ref[0, i] * (adm[0] * arr[0])
            value = value + trans_ref[1, i] * (adm[1] * arr[1])
            value = value + trans_ref[2, i] * (adm[2] * arr[2])
            h_send[step, :, :, i * cases : (i + 1) * cases] = value.reshape(total, cap, cases)
        push_all(h_send, h_recv, 0, step)
        h_recv[step, me] = h_send[step, me]

    fwd[...] = fwd_in[...]
    bwd[...] = bwd_in[...]
    pl.semaphore_wait(barrier, total - 1)

    @pl.loop(1, devs)
    def _(p):
        other = lax.rem(dev + p, devs)
        pltpu.make_async_remote_copy(
            src_ref=imp_ref,
            dst_ref=imp_all.at[dev],
            send_sem=imp_sem.at[0],
            recv_sem=imp_sem.at[1],
            device_id=(area, other),
            device_id_type=MESH,
        ).start()

    gather_send(0)
    imp_all[dev] = imp_ref[...]

    fst = onehot(seg_sub == first_row)
    lst = onehot(seg_sub == last_row)
    gbt[...] = jnp.dot(fst, onehot(slot_lane == slot0_col), preferred_element_type=F32).astype(BF16)
    gft[...] = jnp.dot(lst, onehot(slot_lane == slot1_col), preferred_element_type=F32).astype(BF16)
    not_first = 1.0 - jnp.sum(fst.astype(F32), axis=1, keepdims=True)
    not_last = 1.0 - jnp.sum(lst.astype(F32), axis=1, keepdims=True)
    for m in range(3):
        r = to_column(refl_ref[m : m + 1, :])
        r_next = pltpu.roll(jnp.broadcast_to(r, (segs, cases)), segs - 1, 0)
        keep_f[m] = jnp.broadcast_to((1.0 - r) * not_first, (segs, cases))
        take_f[m] = jnp.broadcast_to(r * not_first, (segs, cases))
        keep_b[m] = (1.0 - r_next) * not_last
        take_b[m] = r_next * not_last
    recv_row = recv_ref[...].astype(F32)
    rsum[...] = onehot(iota((buses, slots), 0).astype(F32) == recv_row)
    rback[...] = onehot(iota((slots, buses), 1).astype(F32) == to_column(recv_row))
    link0, link1 = link_ref[:, 0:1].astype(F32), link_ref[:, 1:2].astype(F32)

    def incidence(d):
        index = (iota((links, buses), 1) + d * buses).astype(F32)
        return jnp.where(index == link0, 1.0, 0.0) - jnp.where(index == link1, 1.0, 0.0)

    ct[...] = incidence(dev).astype(BF16)
    index = (iota((buses, links), 0) + dev * buses).astype(F32)
    cm[...] = (
        jnp.where(index == to_row(link0), 1.0, 0.0) - jnp.where(index == to_row(link1), 1.0, 0.0)
    ).astype(BF16)
    for ij in range(9):
        zcol[ij] = jnp.broadcast_to(to_column(imp_ref[ij : ij + 1, :]), (buses, cases))

    def advance():
        for m in range(3):
            f, b = fwd[m], bwd[m]
            fwd[m] = keep_f[m] * pltpu.roll(f, 1, 0) + take_f[m] * b
            bwd[m] = keep_b[m] * pltpu.roll(b, segs - 1, 0) + take_b[m] * f

    wait(imp_all, devs - 1, imp_sem.at[1])
    minv[...] = jnp.zeros_like(minv)
    eye = iota((links, links), 0) == iota((links, links), 1)

    @pl.loop(0, devs)
    def _(d):
        c = incidence(d)
        for i in range(3):
            for j in range(3):
                z = imp_all[d, 3 * i + j : 3 * i + j + 1, :]
                minv[i * links : (i + 1) * links, j * links : (j + 1) * links] += lax.dot_general(
                    c * z, c, (((1,), (1,)), ((), ())), precision=EXACT, preferred_element_type=F32
                )

    for i in range(3):
        span = slice(i * links, (i + 1) * links)
        minv[span, span] += jnp.where(eye, resist_ref[...], 0.0)
    order = 3 * links
    lane, sub = iota((order, order), 1), iota((order, order), 0)

    @pl.loop(0, 3 * link_real * devs)
    def _(n):
        i, l = n // (link_real * devs), lax.rem(n, link_real * devs)
        k = i * links + (l // link_real) * lp + lax.rem(l, link_real)
        a = minv[...]
        row = minv[pl.ds(k, 1), :]
        here = lane == k
        col = jnp.sum(jnp.where(here, a, 0.0), axis=1, keepdims=True)
        pivot = jnp.sum(jnp.where(lane[:1] == k, row, 0.0), axis=1, keepdims=True)
        inverse = 1.0 / pivot
        scaled_row = row * inverse
        scaled_col = col * inverse
        rest = jnp.where(here, scaled_col, a - col * scaled_row)
        edge = jnp.where(lane[:1] == k, -inverse, scaled_row)
        minv[...] = jnp.where(sub == k, edge, rest)

    def apply(step, values):
        return [
            zcol[3 * i] * values[0] + zcol[3 * i + 1] * values[1] + zcol[3 * i + 2] * values[2]
            for i in range(3)
        ]

    def finish(step):
        advance()
        wait(h_recv.at[step], total - 1, recv_sem.at[0, step])
        for i in range(3):
            part = h_recv[step, :, :, i * cases : (i + 1) * cases].reshape(slots, cases)
            inj[i] = src_ref[step, :, i, :] + pick(rsum[...], part)
        open_volts = apply(step, [inj[i] for i in range(3)])
        for i in range(3):
            e_send[step, :, :, i * cases : (i + 1) * cases] = pick(
                ct[...], open_volts[i]
            ).reshape(devs, lp, cases)
        push_area(lambda other: e_send.at[step, other], e_recv, 1, step)
        e_recv[step, dev] = e_send[step, dev]
        wait(e_recv.at[step], devs - 1, recv_sem.at[1, step])
        g_send[step] = jnp.sum(e_recv[step], axis=0)
        push_area(lambda other: g_send.at[step], g_recv, 2, step)
        g_recv[step, dev] = g_send[step]
        wait(g_recv.at[step], devs - 1, recv_sem.at[2, step])
        stacked = jnp.concatenate(
            [
                g_recv[step, :, :, i * cases : (i + 1) * cases].reshape(links, cases)
                for i in range(3)
            ],
            axis=0,
        )
        current = jnp.dot(minv[...], stacked, precision=EXACT, preferred_element_type=F32)
        net = [
            inj[i] + pick(cm[...], current[i * links : (i + 1) * links]) for i in range(3)
        ]
        volts = apply(step, net)
        for i in range(3):
            volt_ref[step, :, i, :] = volts[i]
            v_send[step, :, :, i * cases : (i + 1) * cases] = pick(rback[...], volts[i]).reshape(
                total, cap, cases
            )
        push_all(v_send, v_recv, 3, step)
        v_recv[step, me] = v_send[step, me]
        wait(v_recv.at[step], total - 1, recv_sem.at[3, step])
        ends = [
            v_recv[step, :, :, i * cases : (i + 1) * cases].reshape(slots, cases) for i in range(3)
        ]
        for m in range(3):
            out = trans_ref[m, 0] * ends[0] + trans_ref[m, 1] * ends[1] + trans_ref[m, 2] * ends[2]
            out = out - arr[m]
            fwd[m] += pick(gbt[...], out)
            bwd[m] += pick(gft[...], out)

    finish(0)

    @pl.loop(1, STEPS)
    def _(step):
        gather_send(step)
        finish(step)

    wait(imp_all, devs - 1, imp_sem.at[0])

    @pl.loop(0, STEPS)
    def _(step):
        wait(h_send.at[step], total - 1, send_sem.at[0, step])
        wait(e_send.at[step], devs - 1, send_sem.at[1, step])
        wait(g_recv.at[step], devs - 1, send_sem.at[2, step])
        wait(v_send.at[step], total - 1, send_sem.at[3, step])


def on_device(
    areas,
    devs,
    wave_fwd,
    wave_bwd,
    seg_reflect,
    seg_count,
    modal_admit,
    modal_transform,
    end_slot,
    recv_bus,
    bus_impedance,
    link_bus,
    link_resist,
    source_current,
):
    total = areas * devs
    cases, segs = wave_fwd.shape[2], wave_fwd.shape[1]
    cap = recv_bus.shape[1] // total
    rows = -(-cap // 8) * 8
    if rows != cap:
        end_slot = end_slot // cap * rows + end_slot % cap
        recv_bus = jnp.pad(
            recv_bus.reshape(total, cap), ((0, 0), (0, rows - cap)), constant_values=-1
        ).reshape(1, total * rows)
    slots = total * rows
    buses = bus_impedance.shape[2]
    link_real = link_bus.shape[0] // devs
    lp = -(-link_real // 8) * 8
    links = lp * devs
    link_pad = jnp.pad(
        link_bus.reshape(devs, link_real, 2),
        ((0, 0), (0, lp - link_real), (0, 0)),
        constant_values=-1,
    ).reshape(links, 2)
    resist_pad = jnp.pad(
        link_resist.reshape(devs, link_real), ((0, 0), (0, lp - link_real)), constant_values=1.0
    ).reshape(links, 1)
    impedance = bus_impedance.reshape(9, buses)
    vmem = pl.BlockSpec(memory_space=pltpu.VMEM)
    smem = pl.BlockSpec(memory_space=pltpu.SMEM)
    wide = 3 * cases
    return pl.pallas_call(
        functools.partial(kernel, areas, devs, link_real),
        out_shape=(
            jax.ShapeDtypeStruct(source_current.shape, F32),
            jax.ShapeDtypeStruct(wave_fwd.shape, F32),
            jax.ShapeDtypeStruct(wave_bwd.shape, F32),
        ),
        in_specs=[vmem] * 5 + [smem] + [vmem] * 6,
        out_specs=(vmem, vmem, vmem),
        scratch_shapes=[
            pltpu.VMEM((STEPS, total, rows, wide), F32),
            pltpu.VMEM((STEPS, total, rows, wide), F32),
            pltpu.VMEM((STEPS, devs, lp, wide), F32),
            pltpu.VMEM((STEPS, devs, lp, wide), F32),
            pltpu.VMEM((STEPS, lp, wide), F32),
            pltpu.VMEM((STEPS, devs, lp, wide), F32),
            pltpu.VMEM((STEPS, total, rows, wide), F32),
            pltpu.VMEM((STEPS, total, rows, wide), F32),
            pltpu.VMEM((devs, 9, buses), F32),
            pltpu.VMEM((slots, segs), BF16),
            pltpu.VMEM((slots, segs), BF16),
            pltpu.VMEM((segs, slots), BF16),
            pltpu.VMEM((segs, slots), BF16),
            pltpu.VMEM((buses, slots), BF16),
            pltpu.VMEM((slots, buses), BF16),
            pltpu.VMEM((links, buses), BF16),
            pltpu.VMEM((buses, links), BF16),
            pltpu.VMEM((3, slots, cases), F32),
            pltpu.VMEM((9, buses, cases), F32),
            pltpu.VMEM((3, segs, cases), F32),
            pltpu.VMEM((3, segs, cases), F32),
            pltpu.VMEM((3, segs, cases), F32),
            pltpu.VMEM((3, segs, cases), F32),
            pltpu.VMEM((3, slots, cases), F32),
            pltpu.VMEM((3, buses, cases), F32),
            pltpu.VMEM((3 * links, 3 * links), F32),
            pltpu.SemaphoreType.DMA((4, STEPS)),
            pltpu.SemaphoreType.DMA((4, STEPS)),
            pltpu.SemaphoreType.DMA((2,)),
        ],
        compiler_params=pltpu.CompilerParams(
            collective_id=0, has_side_effects=True, vmem_limit_bytes=60 * 1024 * 1024
        ),
        name="transient",
    )(
        wave_fwd,
        wave_bwd,
        seg_reflect,
        seg_count,
        modal_admit,
        modal_transform,
        end_slot,
        recv_bus,
        impedance,
        link_pad,
        resist_pad,
        source_current,
    )


def solution(mesh):
    in_specs = (
        P(None, ("area", "dev"), None),
        P(None, ("area", "dev"), None),
        P(None, ("area", "dev")),
        P(("area", "dev"), None),
        P(None, ("area", "dev")),
        P(),
        P(("area", "dev"), None),
        P(("area", "dev"), None),
        P(None, None, ("area", "dev")),
        P("area", None),
        P("area"),
        P(None, ("area", "dev"), None, None),
    )
    out_specs = (
        P(None, ("area", "dev"), None, None),
        P(None, ("area", "dev"), None),
        P(None, ("area", "dev"), None),
    )
    return jax.shard_map(
        functools.partial(on_device, mesh.shape["area"], mesh.shape["dev"]),
        mesh=mesh,
        in_specs=in_specs,
        out_specs=out_specs,
        check_vma=False,
    )
```

time: 497 us -> 158 us (0.32)
  waiting for transfers between devices: 174 us -> 0 us
  Pallas kernels: 0 us -> 145 us
  blocking collectives: 87.2 us -> 0 us
  other arithmetic: 76.1 us -> 0 us
  local copies, waits for them, and re-layouts: 69.5 us -> 9.91 us
  matrix products: 39.5 us -> 0 us
  starting transfers between devices: 27.3 us -> 0 us
  between operations: 17.3 us -> 0.67 us
    pallas_call x0 -> x1, Pallas kernels: none -> 145 us  [on_device(): pl.pallas_call(functools.partial(kernel, areas, devs, link_real), out_sha...]
    unnamed x9 -> x0, waiting for transfers between devices: 106 us -> none
    psum x1 -> x0, waiting for transfers between devices: 50.8 us -> none  [on_device(): lax.psum(partial_value, 'dev') + jnp.diag(jnp.repeat(link_resist, 3))]
    all_to_all x3 -> x0, blocking collectives: 50.2 us -> none  [send_ends(): lax.all_to_all(rows, ('area', 'dev'), split_axis=0, concat_axis=0, tiled=...]
    another operation x19 -> x0, other arithmetic: 45.5 us -> none  [the longest x7 24.3 us: on_device(): factor = jnp.linalg.cholesky(matrix)]
    all_gather x4 -> x0, blocking collectives: 37.1 us -> none  [on_device(): lax.all_gather(solve_links(factor, owned), 'dev', axis=1, tiled=True)]
    add x10 -> x0, other arithmetic: 29.2 us -> none  [the longest x4 15.4 us: on_device(): (1.0 - seg_reflect)[:, :, None] * jnp.roll(forward, 1, axis=1)]
    dot_general x33 -> x0, matrix products: 28.3 us -> none  [the longest x4 5.28 us: on_device(): jnp.einsum('mi,lsik->mlsk', modal_transform, end_volts, precision=exact)]
  transfers between devices with their start and end apart: 10 -> 0, of which waited for: 8 -> 0; matrix products, arithmetic and copies ran while one was open for 19% -> 0% of each run, Pallas kernels for 0% -> 0%
where the time goes in v1:
time: 158 us; the launch traced here: 156 us
  Pallas kernels  145 us (92%)
  local copies, waits for them, and re-layouts  9.91 us (6%)
    pallas_call x1, Pallas kernels, on_device(): pl.pallas_call(functools.partial(kernel, areas, devs, link_real), out_sha...  145 us
    unnamed x15, local copies, waits for them, and re-layouts  5.29 us

profile of v1, /device:TPU:0, one launch (start us, length us, event | category | flops | bytes accessed | tf_op | source)
XLA Modules:
  0.0 155.8 jit_solution(2186643552104101919)
XLA Ops:
  0.6 0.0 copy-start.2
  0.6 0.7 reshape.24
  1.4 0.0 copy-done.2
  1.4 0.0 copy-start.3
  1.4 0.6 reshape.21.imp_ref
  2.0 0.1 copy-done.3
  2.1 0.1 reshape.22
  2.1 0.1 copy.26
  2.3 0.6 pad_bitcast_fusion.link_ref
  2.9 0.0 copy-start.4
  2.9 0.7 reshape.26.resist_ref
  3.6 0.0 copy-done.4
  3.6 0.7 copy.20.slot_ref
  4.3 2.1 %copy.23.src_ref = f32[4,64,3,128]{3,2,1,0:T(4,128)} copy(f32[4,64,3,128]{3,1,2,0:T(8,128)} %param.23) | data formatting | bytes 786432 | tf_op args[11]
  6.4 145.2 %transient.1 = (f32[4,64,3,128]{3,2,1,0:T(4,128)}, f32[3,512,128]{2,1,0:T(8,128)}, f32[3,512,128]{2,1,0:T(8,128)}) custom-call(f32[3,512,128]{2,1,0:T(8,128)} %fwd_in.1, f32[3,512,128]{2,1,0:T(8,128)} %bwd_in.1, f32[3,512]{1,0:T(4,128)} %refl_ref.1, s32[1,64]{1,0:T(1,128)} %count_ref.1, f32[3,64]{1,0:T(4,128)} %admit_ref.1, f32[3,3]{1,0:T(4,128)} %trans_ref.1, ...), custom_call_target="tpu_custom_call" | custom-call | tf_op jit(solution)/shard_map/transient/pallas_call | solution.py:387
  151.6 0.0 copy-start.1
  151.6 1.9 %copy.24 = f32[4,64,3,128]{3,1,2,0:T(8,128)} copy(f32[4,64,3,128]{3,2,1,0:T(4,128)} %get-tuple-element.6) | data formatting | bytes 786432 | tf_op jit(solution)/shard_map/transient/pallas_call | solution.py:387
  153.5 0.0 copy-done.1
  153.5 0.0 copy-start
  153.5 0.9 copy.29
  154.4 0.5 copy-done
  154.9 0.9 copy.30
  (1 shorter events, 0.0 us)
Async XLA Ops:
  0.6 0.8 copy-start.2
  1.4 0.7 copy-start.3
  2.9 0.7 copy-start.4
  151.6 1.9 %copy-start.1 = (f32[3,512,128]{2,1,0:T(8,128)S(1)}, f32[3,512,128]{2,1,0:T(8,128)}, u32[]{:S(2)}) copy-start(f32[3,512,128]{2,1,0:T(8,128)} %get-tuple-element.13) | copy-start | bytes 2359300
  153.5 1.4 copy-start

commit v2 on v1

--- a/solution.py
+++ b/solution.py
@@ -47,7 +47,6 @@
 def kernel(
     areas,
     devs,
-    link_real,
     fwd_in,
     bwd_in,
     refl_ref,
@@ -67,7 +66,6 @@
     h_recv,
     e_send,
     e_recv,
-    g_send,
     g_recv,
     v_send,
     v_recv,
@@ -98,12 +96,12 @@
     me = area * devs + dev
     cases = fwd.shape[2]
     segs = fwd.shape[1]
-    lines = slot_ref.shape[0]
+    lines = slot_ref.shape[1]
     slots = recv_ref.shape[1]
-    buses = imp_ref.shape[1]
-    links = link_ref.shape[0]
+    buses = imp_ref.shape[2]
+    links = link_ref.shape[1]
+    owners = links // 8
     cap = slots // total
-    lp = links // devs
 
     barrier = pltpu.get_barrier_semaphore()
 
@@ -129,15 +127,33 @@
                 device_id_type=MESH,
             ).start()
 
-    def push_area(source, recv, phase, step):
+    def push_shares(step):
+        @pl.loop(0, owners)
+        def _(other):
+            @pl.when(other != dev)
+            def _():
+                pltpu.make_async_remote_copy(
+                    src_ref=e_send.at[step, other],
+                    dst_ref=e_recv.at[step, dev],
+                    send_sem=send_sem.at[1, step],
+                    recv_sem=recv_sem.at[1, step],
+                    device_id=(area, other),
+                    device_id_type=MESH,
+                ).start()
+
+    def sum_shares(step):
+        e_recv[step, dev] = e_send[step, dev]
+        wait(e_recv.at[step], devs - 1, recv_sem.at[1, step])
+        g_recv[step, dev] = jnp.sum(e_recv[step], axis=0)
+
         @pl.loop(1, devs)
         def _(p):
             other = lax.rem(dev + p, devs)
             pltpu.make_async_remote_copy(
-                src_ref=source(other),
-                dst_ref=recv.at[step, dev],
-                send_sem=send_sem.at[phase, step],
-                recv_sem=recv_sem.at[phase, step],
+                src_ref=g_recv.at[step, dev],
+                dst_ref=g_recv.at[step, dev],
+                send_sem=send_sem.at[2, step],
+                recv_sem=recv_sem.at[2, step],
                 device_id=(area, other),
                 device_id_type=MESH,
             ).start()
@@ -155,9 +171,9 @@
     first_row = to_row(first_col)
     last_col = first_col + counts_col - 1.0
     last_row = first_row + counts_row - 1.0
-    slot0_col = slot_ref[:, 0:1].astype(F32)
-    slot1_col = slot_ref[:, 1:2].astype(F32)
-    slot0_row, slot1_row = to_row(slot0_col), to_row(slot1_col)
+    slot0_row = slot_ref[0:1, :].astype(F32)
+    slot1_row = slot_ref[1:2, :].astype(F32)
+    slot0_col, slot1_col = to_column(slot0_row), to_column(slot1_row)
     seg_lane = iota((lines, segs), 1).astype(F32)
     seg_sub = iota((segs, lines), 0).astype(F32)
     slot_lane = iota((lines, slots), 1).astype(F32)
@@ -216,7 +232,8 @@
     recv_row = recv_ref[...].astype(F32)
     rsum[...] = onehot(iota((buses, slots), 0).astype(F32) == recv_row)
     rback[...] = onehot(iota((slots, buses), 1).astype(F32) == to_column(recv_row))
-    link0, link1 = link_ref[:, 0:1].astype(F32), link_ref[:, 1:2].astype(F32)
+    link0_row, link1_row = link_ref[0:1, :].astype(F32), link_ref[1:2, :].astype(F32)
+    link0, link1 = to_column(link0_row), to_column(link1_row)
 
     def incidence(d):
         index = (iota((links, buses), 1) + d * buses).astype(F32)
@@ -225,10 +242,10 @@
     ct[...] = incidence(dev).astype(BF16)
     index = (iota((buses, links), 0) + dev * buses).astype(F32)
     cm[...] = (
-        jnp.where(index == to_row(link0), 1.0, 0.0) - jnp.where(index == to_row(link1), 1.0, 0.0)
+        jnp.where(index == link0_row, 1.0, 0.0) - jnp.where(index == link1_row, 1.0, 0.0)
     ).astype(BF16)
     for ij in range(9):
-        zcol[ij] = jnp.broadcast_to(to_column(imp_ref[ij : ij + 1, :]), (buses, cases))
+        zcol[ij] = jnp.broadcast_to(to_column(imp_ref[ij // 3, ij % 3 : ij % 3 + 1, :]), (buses, cases))
 
     def advance():
         for m in range(3):
@@ -244,8 +261,8 @@
     def _(d):
         c = incidence(d)
         for i in range(3):
-            for j in range(3):
-                z = imp_all[d, 3 * i + j : 3 * i + j + 1, :]
+            for j in range(i + 1):
+                z = imp_all[d, i, j : j + 1, :]
                 minv[i * links : (i + 1) * links, j * links : (j + 1) * links] += lax.dot_general(
                     c * z, c, (((1,), (1,)), ((), ())), precision=EXACT, preferred_element_type=F32
                 )
@@ -253,24 +270,48 @@
     for i in range(3):
         span = slice(i * links, (i + 1) * links)
         minv[span, span] += jnp.where(eye, resist_ref[...], 0.0)
+        for j in range(i):
+            past = slice(j * links, (j + 1) * links)
+            minv[past, span] = minv[span, past]
     order = 3 * links
-    lane, sub = iota((order, order), 1), iota((order, order), 0)
-
-    @pl.loop(0, 3 * link_real * devs)
+    lane = iota((order, order), 1)
+
+    @pl.loop(0, links)
     def _(n):
-        i, l = n // (link_real * devs), lax.rem(n, link_real * devs)
-        k = i * links + (l // link_real) * lp + lax.rem(l, link_real)
+        spots = [n + u * links for u in range(3)]
         a = minv[...]
-        row = minv[pl.ds(k, 1), :]
-        here = lane == k
-        col = jnp.sum(jnp.where(here, a, 0.0), axis=1, keepdims=True)
-        pivot = jnp.sum(jnp.where(lane[:1] == k, row, 0.0), axis=1, keepdims=True)
-        inverse = 1.0 / pivot
-        scaled_row = row * inverse
-        scaled_col = col * inverse
-        rest = jnp.where(here, scaled_col, a - col * scaled_row)
-        edge = jnp.where(lane[:1] == k, -inverse, scaled_row)
-        minv[...] = jnp.where(sub == k, edge, rest)
+        rows = [minv[pl.ds(k, 1), :] for k in spots]
+        here = [lane == k for k in spots]
+        edge = [lane[:1] == k for k in spots]
+        cols = [jnp.sum(jnp.where(h, a, 0.0), axis=1, keepdims=True) for h in here]
+        block = [
+            [jnp.sum(jnp.where(g, r, 0.0), axis=1, keepdims=True) for g in edge] for r in rows
+        ]
+        for v in range(3):
+            inverse = 1.0 / block[v][v]
+            row, col = rows[v], cols[v] * inverse
+            a = a - col * row
+            scaled = row * inverse
+            factor = [block[u][v] for u in range(3)]
+            across = [block[v][w] * inverse for w in range(3)]
+            for u in range(3):
+                rows[u] = scaled if u == v else rows[u] - factor[u] * scaled
+                cols[u] = col if u == v else cols[u] - block[v][u] * col
+            for u in range(3):
+                for w in range(3):
+                    if u != v and w != v:
+                        block[u][w] = block[u][w] - factor[u] * across[w]
+            for u in range(3):
+                if u != v:
+                    block[u][v], block[v][u] = factor[u] * inverse, across[u]
+            block[v][v] = -inverse
+        for u in range(3):
+            a = jnp.where(here[u], cols[u], a)
+            for w in range(3):
+                rows[u] = jnp.where(edge[w], block[u][w], rows[u])
+        minv[...] = a
+        for u in range(3):
+            minv[pl.ds(spots[u], 1), :] = rows[u]
 
     def apply(step, values):
         return [
@@ -283,19 +324,23 @@
         wait(h_recv.at[step], total - 1, recv_sem.at[0, step])
         for i in range(3):
             part = h_recv[step, :, :, i * cases : (i + 1) * cases].reshape(slots, cases)
-            inj[i] = src_ref[step, :, i, :] + pick(rsum[...], part)
+            inj[i] = src_ref[step, i] + pick(rsum[...], part)
         open_volts = apply(step, [inj[i] for i in range(3)])
         for i in range(3):
             e_send[step, :, :, i * cases : (i + 1) * cases] = pick(
                 ct[...], open_volts[i]
-            ).reshape(devs, lp, cases)
-        push_area(lambda other: e_send.at[step, other], e_recv, 1, step)
-        e_recv[step, dev] = e_send[step, dev]
-        wait(e_recv.at[step], devs - 1, recv_sem.at[1, step])
-        g_send[step] = jnp.sum(e_recv[step], axis=0)
-        push_area(lambda other: g_send.at[step], g_recv, 2, step)
-        g_recv[step, dev] = g_send[step]
-        wait(g_recv.at[step], devs - 1, recv_sem.at[2, step])
+            ).reshape(owners, 8, cases)
+        push_shares(step)
+
+        @pl.when(dev < owners)
+        def _():
+            sum_shares(step)
+            wait(g_recv.at[step], owners - 1, recv_sem.at[2, step])
+
+        @pl.when(dev >= owners)
+        def _():
+            wait(g_recv.at[step], owners, recv_sem.at[2, step])
+
         stacked = jnp.concatenate(
             [
                 g_recv[step, :, :, i * cases : (i + 1) * cases].reshape(links, cases)
@@ -309,7 +354,7 @@
         ]
         volts = apply(step, net)
         for i in range(3):
-            volt_ref[step, :, i, :] = volts[i]
+            volt_ref[step, i] = volts[i]
             v_send[step, :, :, i * cases : (i + 1) * cases] = pick(rback[...], volts[i]).reshape(
                 total, cap, cases
             )
@@ -337,8 +382,16 @@
     @pl.loop(0, STEPS)
     def _(step):
         wait(h_send.at[step], total - 1, send_sem.at[0, step])
-        wait(e_send.at[step], devs - 1, send_sem.at[1, step])
-        wait(g_recv.at[step], devs - 1, send_sem.at[2, step])
+
+        @pl.when(dev < owners)
+        def _():
+            wait(e_send.at[step], owners - 1, send_sem.at[1, step])
+            wait(e_recv.at[step], devs - 1, send_sem.at[2, step])
+
+        @pl.when(dev >= owners)
+        def _():
+            wait(e_send.at[step], owners, send_sem.at[1, step])
+
         wait(v_send.at[step], total - 1, send_sem.at[3, step])
 
 
@@ -369,25 +422,14 @@
         ).reshape(1, total * rows)
     slots = total * rows
     buses = bus_impedance.shape[2]
-    link_real = link_bus.shape[0] // devs
-    lp = -(-link_real // 8) * 8
-    links = lp * devs
-    link_pad = jnp.pad(
-        link_bus.reshape(devs, link_real, 2),
-        ((0, 0), (0, lp - link_real), (0, 0)),
-        constant_values=-1,
-    ).reshape(links, 2)
-    resist_pad = jnp.pad(
-        link_resist.reshape(devs, link_real), ((0, 0), (0, lp - link_real)), constant_values=1.0
-    ).reshape(links, 1)
-    impedance = bus_impedance.reshape(9, buses)
+    links = link_bus.shape[0]
     vmem = pl.BlockSpec(memory_space=pltpu.VMEM)
     smem = pl.BlockSpec(memory_space=pltpu.SMEM)
     wide = 3 * cases
-    return pl.pallas_call(
-        functools.partial(kernel, areas, devs, link_real),
+    volts, fwd, bwd = pl.pallas_call(
+        functools.partial(kernel, areas, devs),
         out_shape=(
-            jax.ShapeDtypeStruct(source_current.shape, F32),
+            jax.ShapeDtypeStruct((STEPS, 3, buses, cases), F32),
             jax.ShapeDtypeStruct(wave_fwd.shape, F32),
             jax.ShapeDtypeStruct(wave_bwd.shape, F32),
         ),
@@ -396,13 +438,12 @@
         scratch_shapes=[
             pltpu.VMEM((STEPS, total, rows, wide), F32),
             pltpu.VMEM((STEPS, total, rows, wide), F32),
-            pltpu.VMEM((STEPS, devs, lp, wide), F32),
-            pltpu.VMEM((STEPS, devs, lp, wide), F32),
-            pltpu.VMEM((STEPS, lp, wide), F32),
-            pltpu.VMEM((STEPS, devs, lp, wide), F32),
+            pltpu.VMEM((STEPS, links // 8, 8, wide), F32),
+            pltpu.VMEM((STEPS, devs, 8, wide), F32),
+            pltpu.VMEM((STEPS, links // 8, 8, wide), F32),
             pltpu.VMEM((STEPS, total, rows, wide), F32),
             pltpu.VMEM((STEPS, total, rows, wide), F32),
-            pltpu.VMEM((devs, 9, buses), F32),
+            pltpu.VMEM((devs, 3, 3, buses), F32),
             pltpu.VMEM((slots, segs), BF16),
             pltpu.VMEM((slots, segs), BF16),
             pltpu.VMEM((segs, slots), BF16),
@@ -435,13 +476,14 @@
         seg_count,
         modal_admit,
         modal_transform,
-        end_slot,
+        end_slot.T,
         recv_bus,
-        impedance,
-        link_pad,
-        resist_pad,
-        source_current,
+        bus_impedance,
+        link_bus.T,
+        link_resist.reshape(1, links),
+        jnp.transpose(source_current, (0, 2, 1, 3)),
     )
+    return (jnp.transpose(volts, (0, 2, 1, 3)), fwd, bwd)
 
 
 def solution(mesh):

time: 158 us -> 138 us (0.87)
  Pallas kernels: 145 us -> 131 us
  local copies, waits for them, and re-layouts: 9.91 us -> 4.14 us
    pallas_call x1, Pallas kernels: 145 us -> 131 us  [on_device(): pl.pallas_call(functools.partial(kernel, areas, devs), out_shape=(jax.Sha...]
    reshape x5 -> x0, local copies, waits for them, and re-layouts: 2.71 us -> none  [the longest x1 0.74 us: on_device(): link_resist.reshape(devs, link_real)]
    pallas_call x1 -> x0, local copies, waits for them, and re-layouts: 1.9 us -> none  [on_device(): pl.pallas_call(functools.partial(kernel, areas, devs, link_real), out_sha...]
    unnamed x15 -> x7, local copies, waits for them, and re-layouts: 5.29 us -> 4.14 us
where the time goes in v2:
time: 138 us; the launch traced here: 135 us
  Pallas kernels  131 us (95%)
  local copies, waits for them, and re-layouts  4.14 us (3%)
    pallas_call x1, Pallas kernels, on_device(): pl.pallas_call(functools.partial(kernel, areas, devs), out_shape=(jax.Sha...  131 us
    unnamed x7, local copies, waits for them, and re-layouts  4.14 us

profile of v2, /device:TPU:0, one launch (start us, length us, event | category | flops | bytes accessed | tf_op | source)
XLA Modules:
  0.0 135.5 jit_solution(13192479814903070906)
XLA Ops:
  0.6 130.7 %transient.1 = (f32[4,3,64,128]{3,2,1,0:T(8,128)}, f32[3,512,128]{2,1,0:T(8,128)}, f32[3,512,128]{2,1,0:T(8,128)}) custom-call(f32[3,512,128]{2,1,0:T(8,128)} %fwd_in.1, f32[3,512,128]{2,1,0:T(8,128)} %bwd_in.1, f32[3,512]{1,0:T(4,128)} %refl_ref.1, s32[1,64]{1,0:T(1,128)} %count_ref.1, f32[3,64]{1,0:T(4,128)} %admit_ref.1, f32[3,3]{1,0:T(4,128)} %trans_ref.1, ...), custom_call_target="tpu_custom_call" | custom-call | tf_op jit(solution)/shard_map/transient/pallas_call | solution.py:429
  131.3 0.0 copy-start.1
  131.3 1.8 %copy.18 = f32[4,64,3,128]{3,1,2,0:T(8,128)} copy(f32[4,64,3,128]{3,1,2,0:T(8,128)} %bitcast.5) | data formatting | bytes 786432
  133.2 0.0 copy-done.1
  133.2 0.0 copy-start
  133.2 0.9 copy.19
  134.0 0.5 copy-done
  134.6 0.9 copy.20
Async XLA Ops:
  131.3 1.9 %copy-start.1 = (f32[3,512,128]{2,1,0:T(8,128)S(1)}, f32[3,512,128]{2,1,0:T(8,128)}, u32[]{:S(2)}) copy-start(f32[3,512,128]{2,1,0:T(8,128)} %get-tuple-element.13) | copy-start | bytes 2359300
  133.2 1.4 %copy-start = (f32[3,512,128]{2,1,0:T(8,128)S(1)}, f32[3,512,128]{2,1,0:T(8,128)}, u32[]{:S(2)}) copy-start(f32[3,512,128]{2,1,0:T(8,128)} %get-tuple-element.14) | copy-start | bytes 2359300
